TPU v7x, 32 devices: a whole 2x2x4 slice. The times are simulated.
32 devices in a mesh: blk: 8 (over z, y), shard: 4 (over x, core).
Axes of the slice: x: 2, y: 2, z: 4, core: 2. Of those that a mesh axis runs over, the one named last changes fastest.
Arguments:
- weights: bfloat16 [8, 8192, 2048], P('blk', 'shard'), may hold values from -90 to 90
- warm_factor: float32 [8, 32, 2048], P('blk'), may hold values from -6 to 6
Outputs:
- new_weights: bfloat16 [8, 8192, 2048], P('blk', 'shard')
- new_factor: float32 [8, 32, 2048], P('blk', None, 'shard')
All inputs are finite; a program needn't handle non-finite values.
Results may differ from a plain program's by a relative error of at most 0.012.
Values may be sent and summed in bfloat16 or wider, within the bound.
No kernel may reach another device: no remote copies, remote signals or barrier semaphores. Data moves between devices by JAX's collectives and lax.ppermute only.
A program may use at most 64 MiB of HBM per device.

v0:
```python
import jax
import jax.numpy as jnp
from jax import lax
from jax.sharding import PartitionSpec as P

POWER = 4
MIXING = 1.0 / 3.0


def passed_along(value, axis, by):
    peers = lax.axis_size(axis)
    return lax.ppermute(value, axis, [(i, (i + by) % peers) for i in range(peers)])


def lower_solve(lower_factor, right_hand):
    return jax.scipy.linalg.solve_triangular(lower_factor, right_hand, lower=True)


def on_device(weights, warm_factor):
    local_weight = weights[0]
    own_factor = warm_factor[0]
    own_rounded = own_factor.astype(jnp.bfloat16)
    prior_rounded = passed_along(own_rounded, "blk", 1)
    rounded = jnp.stack([own_rounded, prior_rounded])
    width_piece = local_weight.shape[1] // lax.axis_size("shard")
    own_piece = jnp.stack([own_factor, own_factor])[:, :, :width_piece]
    left_rows = jnp.zeros((2, own_factor.shape[0], local_weight.shape[0]), jnp.bfloat16)
    for iteration in range(POWER):
        products = jnp.einsum(
            "ekc,rc->ekr", rounded, local_weight, preferred_element_type=jnp.float32
        )
        from_next = passed_along(products[1], "blk", -1)
        from_prior = passed_along(products[0], "blk", 1)
        raw_factor = jnp.stack([products[0] - from_next, from_prior - products[1]])
        gram = jnp.einsum("ekr,elr->ekl", raw_factor, raw_factor, precision=lax.Precision.HIGHEST)
        gram = lax.psum(gram, "shard")
        lower_factor = jnp.linalg.cholesky(gram)
        basis = jax.vmap(lower_solve)(lower_factor, raw_factor)
        left_rows = basis.astype(jnp.bfloat16)
        partials = jnp.einsum(
            "ekr,rc->ekc", left_rows, local_weight, preferred_element_type=jnp.float32
        )
        next_part = passed_along(partials[1], "blk", -1)
        prior_part = passed_along(partials[0], "blk", 1)
        factors = lax.psum(jnp.stack([partials[0] - next_part, prior_part - partials[1]]), "shard")
        own_piece = lax.dynamic_slice_in_dim(
            factors, lax.axis_index("shard") * width_piece, width_piece, 2
        )
        rounded = factors.astype(jnp.bfloat16)
    signed = jnp.concatenate([left_rows[1], -left_rows[0]], axis=0)
    factor_pair = jnp.concatenate([rounded[1], rounded[0]], axis=0)
    delta = jnp.einsum("jr,jc->rc", signed, factor_pair, preferred_element_type=jnp.float32)
    new_weight = (local_weight.astype(jnp.float32) + MIXING * delta).astype(jnp.bfloat16)
    return (new_weight[None], own_piece[0][None])


def solution(mesh):
    placed = (P("blk", "shard", None), P("blk", None, None))
    return jax.shard_map(
        on_device,
        mesh=mesh,
        in_specs=placed,
        out_specs=(P("blk", "shard", None), P("blk", None, "shard")),
        check_vma=False,
    )
```

profile of v0, /device:TPU:0, one launch (start us, length us, event | category | flops | bytes accessed | tf_op | source)
XLA Modules:
  0.0 363.7 jit_solution(13797275258302766750)
XLA Ops:
  17.7 6.0 %fusion.14 = f32[2,32,2048]{2,1,0:T(8,128)S(1)} fusion(bf16[1,2048,2048]{2,1,0:T(8,128)(2,1)} %param.5, bf16[1,32,2048]{2,1,0:T(8,128)(2,1)S(1)} %bitcast.173, bf16[1,32,2048]{2,1,0:T(8,128)(2,1)S(1)} %convert_element_type.38), kind=kOutput, calls=%fused_computation.15 | convolution fusion | flops 537001984 | bytes 9175040 | tf_op jit(solution)/shard_map/ekc,rc->ekr/dot_general | solution.py:29
  25.9 11.1 %collective-permute-done.1 = f32[32,2048]{1,0:T(8,128)S(1)} collective-permute-done((f32[32,2048]{1,0:T(8,128)S(1)}, f32[32,2048]{1,0:T(8,128)S(1)}, u32[]{:S(2)}, u32[]{:S(2)}) %collective-permute-start.1) | collective-permute-done | bytes 262176 | tf_op jit(solution)/shard_map/ppermute | solution.py:12
  37.6 10.3 %psum.56 = f32[2,32,32]{1,2,0:T(8,128)S(1)} all-reduce(f32[2,32,32]{1,2,0:T(8,128)S(1)} %fusion.20), channel_id=1, replica_groups=mesh['blk'=8,'shard'=4] {'shard'}, use_global_device_ids=true, to_apply=%region_0.0 | all-reduce | flops 2048 | bytes 16384 | tf_op jit(solution)/shard_map/psum | solution.py:36
  48.0 5.9 %custom-call.12 = f32[2,32,32]{2,1,0:T(8,128)S(1)} custom-call(f32[2,32,32]{2,1,0:T(8,128)S(1)} %fusion.41), custom_call_target="Cholesky" | custom-call | tf_op jit(solution)/shard_map/jit(cholesky)/cholesky | solution.py:37
  67.2 11.4 %collective-permute-done.3 = f32[32,2048]{1,0:T(8,128)S(1)} collective-permute-done((f32[32,2048]{1,0:T(8,128)S(1)}, f32[32,2048]{1,0:T(8,128)S(1)}, u32[]{:S(2)}, u32[]{:S(2)}) %collective-permute-start.3) | collective-permute-done | bytes 262176 | tf_op jit(solution)/shard_map/ppermute | solution.py:12
  78.8 16.0 %all-reduce.6 = bf16[2,32,2048]{2,1,0:T(8,128)(2,1)S(1)} all-reduce(f32[2,32,2048]{2,1,0:T(8,128)S(1)} %pad_maximum_fusion.1), channel_id=1, replica_groups=mesh['blk'=8,'shard'=4] {'shard'}, use_global_device_ids=true, to_apply=%region_3.0 | all-reduce | flops 131072 | bytes 786432 | tf_op jit(solution)/shard_map/psum | solution.py:45
  94.7 6.0 %fusion.10 = f32[2,32,2048]{2,1,0:T(8,128)S(1)} fusion(bf16[1,2048,2048]{2,1,0:T(8,128)(2,1)} %param.5, bf16[2,32,2048]{2,1,0:T(8,128)(2,1)S(1)} %all-reduce.6), kind=kOutput, calls=%fused_computation.11 | convolution fusion | flops 536870912 | bytes 9175040 | tf_op jit(solution)/shard_map/ekc,rc->ekr/dot_general | solution.py:29
  114.9 10.3 %psum.58 = f32[2,32,32]{1,2,0:T(8,128)S(1)} all-reduce(f32[2,32,32]{1,2,0:T(8,128)S(1)} %fusion.19), channel_id=1, replica_groups=mesh['blk'=8,'shard'=4] {'shard'}, use_global_device_ids=true, to_apply=%region_4.0 | all-reduce | flops 2048 | bytes 16384 | tf_op jit(solution)/shard_map/psum | solution.py:36
  125.3 5.9 %custom-call.14 = f32[2,32,32]{2,1,0:T(8,128)S(1)} custom-call(f32[2,32,32]{2,1,0:T(8,128)S(1)} %fusion.39), custom_call_target="Cholesky" | custom-call | tf_op jit(solution)/shard_map/jit(cholesky)/cholesky | solution.py:37
  145.5 10.6 %collective-permute-done.7 = f32[32,2048]{1,0:T(8,128)S(1)} collective-permute-done((f32[32,2048]{1,0:T(8,128)S(1)}, f32[32,2048]{1,0:T(8,128)S(1)}, u32[]{:S(2)}, u32[]{:S(2)}) %collective-permute-start.7) | collective-permute-done | bytes 262176 | tf_op jit(solution)/shard_map/ppermute | solution.py:12
  156.3 16.8 %all-reduce.7 = bf16[2,32,2048]{2,1,0:T(8,128)(2,1)S(1)} all-reduce(f32[2,32,2048]{2,1,0:T(8,128)S(1)} %pad_maximum_fusion.3), channel_id=1, replica_groups=mesh['blk'=8,'shard'=4] {'shard'}, use_global_device_ids=true, to_apply=%region_5.0 | all-reduce | flops 131072 | bytes 786432 | tf_op jit(solution)/shard_map/psum | solution.py:45
  173.1 6.0 %fusion.6 = f32[2,32,2048]{2,1,0:T(8,128)S(1)} fusion(bf16[1,2048,2048]{2,1,0:T(8,128)(2,1)} %param.5, bf16[2,32,2048]{2,1,0:T(8,128)(2,1)S(1)} %all-reduce.7), kind=kOutput, calls=%fused_computation.7 | convolution fusion | flops 536870912 | bytes 9175040 | tf_op jit(solution)/shard_map/ekc,rc->ekr/dot_general | solution.py:29
  181.8 11.8 %collective-permute-done.9 = f32[32,2048]{1,0:T(8,128)S(1)} collective-permute-done((f32[32,2048]{1,0:T(8,128)S(1)}, f32[32,2048]{1,0:T(8,128)S(1)}, u32[]{:S(2)}, u32[]{:S(2)}) %collective-permute-start.9) | collective-permute-done | bytes 262176 | tf_op jit(solution)/shard_map/ppermute | solution.py:12
  194.2 10.5 %psum.60 = f32[2,32,32]{1,2,0:T(8,128)S(1)} all-reduce(f32[2,32,32]{1,2,0:T(8,128)S(1)} %fusion.18), channel_id=1, replica_groups=mesh['blk'=8,'shard'=4] {'shard'}, use_global_device_ids=true, to_apply=%region_6.0 | all-reduce | flops 2048 | bytes 16384 | tf_op jit(solution)/shard_map/psum | solution.py:36
  204.8 5.9 %custom-call.16 = f32[2,32,32]{2,1,0:T(8,128)S(1)} custom-call(f32[2,32,32]{2,1,0:T(8,128)S(1)} %fusion.37), custom_call_target="Cholesky" | custom-call | tf_op jit(solution)/shard_map/jit(cholesky)/cholesky | solution.py:37
  223.6 11.3 %collective-permute-done.11 = f32[32,2048]{1,0:T(8,128)S(1)} collective-permute-done((f32[32,2048]{1,0:T(8,128)S(1)}, f32[32,2048]{1,0:T(8,128)S(1)}, u32[]{:S(2)}, u32[]{:S(2)}) %collective-permute-start.11) | collective-permute-done | bytes 262176 | tf_op jit(solution)/shard_map/ppermute | solution.py:12
  235.0 15.9 %all-reduce.8 = bf16[2,32,2048]{2,1,0:T(8,128)(2,1)S(1)} all-reduce(f32[2,32,2048]{2,1,0:T(8,128)S(1)} %pad_maximum_fusion.5), channel_id=1, replica_groups=mesh['blk'=8,'shard'=4] {'shard'}, use_global_device_ids=true, to_apply=%region_7.0 | all-reduce | flops 131072 | bytes 786432 | tf_op jit(solution)/shard_map/psum | solution.py:45
  250.9 6.0 %fusion.2 = f32[2,32,2048]{2,1,0:T(8,128)S(1)} fusion(bf16[1,2048,2048]{2,1,0:T(8,128)(2,1)} %param.5, bf16[2,32,2048]{2,1,0:T(8,128)(2,1)S(1)} %all-reduce.8), kind=kOutput, calls=%fused_computation.3 | convolution fusion | flops 536870912 | bytes 9175040 | tf_op jit(solution)/shard_map/ekc,rc->ekr/dot_general | solution.py:29
  260.0 11.2 %collective-permute-done.13 = f32[32,2048]{1,0:T(8,128)S(1)} collective-permute-done((f32[32,2048]{1,0:T(8,128)S(1)}, f32[32,2048]{1,0:T(8,128)S(1)}, u32[]{:S(2)}, u32[]{:S(2)}) %collective-permute-start.13) | collective-permute-done | bytes 262176 | tf_op jit(solution)/shard_map/ppermute | solution.py:12
  271.8 10.8 %psum.62 = f32[2,32,32]{1,2,0:T(8,128)S(1)} all-reduce(f32[2,32,32]{1,2,0:T(8,128)S(1)} %fusion.17), channel_id=1, replica_groups=mesh['blk'=8,'shard'=4] {'shard'}, use_global_device_ids=true, to_apply=%region_8.11 | all-reduce | flops 2048 | bytes 16384 | tf_op jit(solution)/shard_map/psum | solution.py:36
  282.7 5.9 %custom-call.18 = f32[2,32,32]{2,1,0:T(8,128)S(1)} custom-call(f32[2,32,32]{2,1,0:T(8,128)S(1)} %fusion.35), custom_call_target="Cholesky" | custom-call | tf_op jit(solution)/shard_map/jit(cholesky)/cholesky | solution.py:37
  302.9 10.7 %collective-permute-done.15 = f32[32,2048]{1,0:T(8,128)S(1)} collective-permute-done((f32[32,2048]{1,0:T(8,128)S(1)}, f32[32,2048]{1,0:T(8,128)S(1)}, u32[]{:S(2)}, u32[]{:S(2)}) %collective-permute-start.15) | collective-permute-done | bytes 262176 | tf_op jit(solution)/shard_map/ppermute | solution.py:12
  314.6 32.8 %all-reduce.5.cloned.1.call-done = f32[2,32,2048]{2,1,0:T(8,128)} async-done(((f32[2,32,2048]{2,1,0:T(8,128)}), f32[2,32,2048]{2,1,0:T(8,128)}) %all-reduce.5.cloned.1.call-update) | async-done | bytes 524304 | tf_op jit(solution)/shard_map/psum | solution.py:45
  348.5 6.9 %fusion.16 = bf16[1,2048,2048]{2,1,0:T(8,128)(2,1)} fusion(bf16[1,2048,2048]{2,1,0:T(8,128)(2,1)} %param.5, bf16[32,2048]{1,0:T(8,128)(2,1)S(1)} %get-tuple-element.39, bf16[32,2048]{1,0:T(8,128)(2,1)S(1)} %get-tuple-element.38, bf16[32,2048]{1,0:T(8,128)(2,1)S(1)} %get-tuple-element.37, bf16[32,2048]{1,0:T(8,128)(2,1)S(1)} %get-tuple-element.36), kind=kOutput, calls=%fused_computation.17 | convolution fusion | flops 554696704 | bytes 17301504 | tf_op jit(solution)/shard_map/jr,jc->rc/dot_general | solution.py:52
  (93 shorter events, 93.6 us)
Async XLA Ops:
  7.2 340.2 %all-reduce.5.cloned.1.call-start = ((), (), s32[]{:S(2)}) async-start(), calls=%async_computation | async-start | bytes 1048576 | tf_op jit(solution)/shard_map/psum | solution.py:45
  8.2 9.6 %collective-permute-start = (bf16[32,2048]{1,0:T(8,128)(2,1)S(1)}, bf16[32,2048]{1,0:T(8,128)(2,1)S(1)}, u32[]{:S(2)}, u32[]{:S(2)}) collective-permute-start(bf16[32,2048]{1,0:T(8,128)(2,1)S(1)} %convert_bitcast_fusion), channel_id=1, source_target_pairs={{0,4},{4,8},{8,12},{12,16},{16,20},{20,24},{24,28},{28,0},{1,5},{5... | collective-permute-start | bytes 393224 | tf_op jit(solution)/shard_map/ppermute | solution.py:12
  23.8 13.2 %collective-permute-start.1 = (f32[32,2048]{1,0:T(8,128)S(1)}, f32[32,2048]{1,0:T(8,128)S(1)}, u32[]{:S(2)}, u32[]{:S(2)}) collective-permute-start(f32[32,2048]{1,0:T(8,128)S(1)} %get-tuple-element.34), channel_id=1, source_target_pairs={{0,28},{4,0},{8,4},{12,8},{16,12},{20,16},{24,20},{28,24},{1,29},{... | collective-permute-start | bytes 786440 | tf_op jit(solution)/shard_map/ppermute | solution.py:12
  25.6 11.4 %collective-permute-start.2 = (f32[32,2048]{1,0:T(8,128)S(1)}, f32[32,2048]{1,0:T(8,128)S(1)}, u32[]{:S(2)}, u32[]{:S(2)}) collective-permute-start(f32[32,2048]{1,0:T(8,128)S(1)} %get-tuple-element.35), channel_id=1, source_target_pairs={{0,4},{4,8},{8,12},{12,16},{16,20},{20,24},{24,28},{28,0},{1,5},{5... | collective-permute-start | bytes 786440 | tf_op jit(solution)/shard_map/ppermute | solution.py:12
  64.6 14.0 %collective-permute-start.3 = (f32[32,2048]{1,0:T(8,128)S(1)}, f32[32,2048]{1,0:T(8,128)S(1)}, u32[]{:S(2)}, u32[]{:S(2)}) collective-permute-start(f32[32,2048]{1,0:T(8,128)S(1)} %get-tuple-element.30), channel_id=1, source_target_pairs={{0,28},{4,0},{8,4},{12,8},{16,12},{20,16},{24,20},{28,24},{1,29},{... | collective-permute-start | bytes 786440 | tf_op jit(solution)/shard_map/ppermute | solution.py:12
  67.2 11.4 %collective-permute-start.4 = (f32[32,2048]{1,0:T(8,128)S(1)}, f32[32,2048]{1,0:T(8,128)S(1)}, u32[]{:S(2)}, u32[]{:S(2)}) collective-permute-start(f32[32,2048]{1,0:T(8,128)S(1)} %get-tuple-element.31), channel_id=1, source_target_pairs={{0,4},{4,8},{8,12},{12,16},{16,20},{20,24},{24,28},{28,0},{1,5},{5... | collective-permute-start | bytes 786440 | tf_op jit(solution)/shard_map/ppermute | solution.py:12
  100.8 8.6 %collective-permute-start.5 = (f32[32,2048]{1,0:T(8,128)S(1)}, f32[32,2048]{1,0:T(8,128)S(1)}, u32[]{:S(2)}, u32[]{:S(2)}) collective-permute-start(f32[32,2048]{1,0:T(8,128)S(1)} %get-tuple-element.26), channel_id=1, source_target_pairs={{0,28},{4,0},{8,4},{12,8},{16,12},{20,16},{24,20},{28,24},{1,29},{... | collective-permute-start | bytes 786440 | tf_op jit(solution)/shard_map/ppermute | solution.py:12
  103.6 10.7 %collective-permute-start.6 = (f32[32,2048]{1,0:T(8,128)S(1)}, f32[32,2048]{1,0:T(8,128)S(1)}, u32[]{:S(2)}, u32[]{:S(2)}) collective-permute-start(f32[32,2048]{1,0:T(8,128)S(1)} %get-tuple-element.27), channel_id=1, source_target_pairs={{0,4},{4,8},{8,12},{12,16},{16,20},{20,24},{24,28},{28,0},{1,5},{5... | collective-permute-start | bytes 786440 | tf_op jit(solution)/shard_map/ppermute | solution.py:12
  142.0 14.1 %collective-permute-start.7 = (f32[32,2048]{1,0:T(8,128)S(1)}, f32[32,2048]{1,0:T(8,128)S(1)}, u32[]{:S(2)}, u32[]{:S(2)}) collective-permute-start(f32[32,2048]{1,0:T(8,128)S(1)} %get-tuple-element.22), channel_id=1, source_target_pairs={{0,28},{4,0},{8,4},{12,8},{16,12},{20,16},{24,20},{28,24},{1,29},{... | collective-permute-start | bytes 786440 | tf_op jit(solution)/shard_map/ppermute | solution.py:12
  145.5 10.7 %collective-permute-start.8 = (f32[32,2048]{1,0:T(8,128)S(1)}, f32[32,2048]{1,0:T(8,128)S(1)}, u32[]{:S(2)}, u32[]{:S(2)}) collective-permute-start(f32[32,2048]{1,0:T(8,128)S(1)} %get-tuple-element.23), channel_id=1, source_target_pairs={{0,4},{4,8},{8,12},{12,16},{16,20},{20,24},{24,28},{28,0},{1,5},{5... | collective-permute-start | bytes 786440 | tf_op jit(solution)/shard_map/ppermute | solution.py:12
  179.2 14.4 %collective-permute-start.9 = (f32[32,2048]{1,0:T(8,128)S(1)}, f32[32,2048]{1,0:T(8,128)S(1)}, u32[]{:S(2)}, u32[]{:S(2)}) collective-permute-start(f32[32,2048]{1,0:T(8,128)S(1)} %get-tuple-element.18), channel_id=1, source_target_pairs={{0,28},{4,0},{8,4},{12,8},{16,12},{20,16},{24,20},{28,24},{1,29},{... | collective-permute-start | bytes 786440 | tf_op jit(solution)/shard_map/ppermute | solution.py:12
  181.7 11.9 %collective-permute-start.10 = (f32[32,2048]{1,0:T(8,128)S(1)}, f32[32,2048]{1,0:T(8,128)S(1)}, u32[]{:S(2)}, u32[]{:S(2)}) collective-permute-start(f32[32,2048]{1,0:T(8,128)S(1)} %get-tuple-element.19), channel_id=1, source_target_pairs={{0,4},{4,8},{8,12},{12,16},{16,20},{20,24},{24,28},{28,0},{1,5},{5... | collective-permute-start | bytes 786440 | tf_op jit(solution)/shard_map/ppermute | solution.py:12
  221.5 13.4 %collective-permute-start.11 = (f32[32,2048]{1,0:T(8,128)S(1)}, f32[32,2048]{1,0:T(8,128)S(1)}, u32[]{:S(2)}, u32[]{:S(2)}) collective-permute-start(f32[32,2048]{1,0:T(8,128)S(1)} %get-tuple-element.14), channel_id=1, source_target_pairs={{0,28},{4,0},{8,4},{12,8},{16,12},{20,16},{24,20},{28,24},{1,29},{... | collective-permute-start | bytes 786440 | tf_op jit(solution)/shard_map/ppermute | solution.py:12
  223.2 11.7 %collective-permute-start.12 = (f32[32,2048]{1,0:T(8,128)S(1)}, f32[32,2048]{1,0:T(8,128)S(1)}, u32[]{:S(2)}, u32[]{:S(2)}) collective-permute-start(f32[32,2048]{1,0:T(8,128)S(1)} %get-tuple-element.15), channel_id=1, source_target_pairs={{0,4},{4,8},{8,12},{12,16},{16,20},{20,24},{24,28},{28,0},{1,5},{5... | collective-permute-start | bytes 786440 | tf_op jit(solution)/shard_map/ppermute | solution.py:12
  257.0 14.2 %collective-permute-start.13 = (f32[32,2048]{1,0:T(8,128)S(1)}, f32[32,2048]{1,0:T(8,128)S(1)}, u32[]{:S(2)}, u32[]{:S(2)}) collective-permute-start(f32[32,2048]{1,0:T(8,128)S(1)} %get-tuple-element.10), channel_id=1, source_target_pairs={{0,28},{4,0},{8,4},{12,8},{16,12},{20,16},{24,20},{28,24},{1,29},{... | collective-permute-start | bytes 786440 | tf_op jit(solution)/shard_map/ppermute | solution.py:12
  260.0 11.2 %collective-permute-start.14 = (f32[32,2048]{1,0:T(8,128)S(1)}, f32[32,2048]{1,0:T(8,128)S(1)}, u32[]{:S(2)}, u32[]{:S(2)}) collective-permute-start(f32[32,2048]{1,0:T(8,128)S(1)} %get-tuple-element.11), channel_id=1, source_target_pairs={{0,4},{4,8},{8,12},{12,16},{16,20},{20,24},{24,28},{28,0},{1,5},{5... | collective-permute-start | bytes 786440 | tf_op jit(solution)/shard_map/ppermute | solution.py:12
  299.4 14.1 %collective-permute-start.15 = (f32[32,2048]{1,0:T(8,128)S(1)}, f32[32,2048]{1,0:T(8,128)S(1)}, u32[]{:S(2)}, u32[]{:S(2)}) collective-permute-start(f32[32,2048]{1,0:T(8,128)S(1)} %get-tuple-element.6), channel_id=1, source_target_pairs={{0,28},{4,0},{8,4},{12,8},{16,12},{20,16},{24,20},{28,24},{1,29},{... | collective-permute-start | bytes 786440 | tf_op jit(solution)/shard_map/ppermute | solution.py:12
  302.9 10.8 %collective-permute-start.16 = (f32[32,2048]{1,0:T(8,128)S(1)}, f32[32,2048]{1,0:T(8,128)S(1)}, u32[]{:S(2)}, u32[]{:S(2)}) collective-permute-start(f32[32,2048]{1,0:T(8,128)S(1)} %get-tuple-element.7), channel_id=1, source_target_pairs={{0,4},{4,8},{8,12},{12,16},{16,20},{20,24},{24,28},{28,0},{1,5},{5... | collective-permute-start | bytes 786440 | tf_op jit(solution)/shard_map/ppermute | solution.py:12
Sparse Core Ops, SparseCore 0:
  314.7 32.6 all-reduce.4
where the time goes:
time: 364 us
  waiting for transfers between devices  127 us (35%)
  blocking collectives  90.5 us (25%)
  matrix products  55.7 us (15%)
  other arithmetic  48.5 us (13%)
  starting transfers between devices  25.1 us (7%)
  between operations  14.3 us (4%)
    ppermute x17, waiting for transfers between devices, passed_along(): lax.ppermute(value, axis, [(i, (i + by) % peers) for i in range(peers)])  94.6 us
    psum x3, blocking collectives, on_device(): lax.psum(jnp.stack([partials[0] - next_part, prior_part - partials[1]]),...  48.7 us
    psum x4, blocking collectives, on_device(): gram = lax.psum(gram, 'shard')  41.9 us
    psum x1, waiting for transfers between devices, on_device(): lax.psum(jnp.stack([partials[0] - next_part, prior_part - partials[1]]),...  32.8 us
    ppermute x17, starting transfers between devices, passed_along(): lax.ppermute(value, axis, [(i, (i + by) % peers) for i in range(peers)])  25.1 us
    dot_general x4, matrix products, on_device(): jnp.einsum('ekc,rc->ekr', rounded, local_weight, preferred_element_type=j...  24.1 us
    another operation x13, other arithmetic, on_device(): lower_factor = jnp.linalg.cholesky(gram)  24.1 us
    another operation x9, other arithmetic, lower_solve(): jax.scipy.linalg.solve_triangular(lower_factor, right_hand, lower=True)  20 us
  transfers between devices with their start and end apart: 18, of which 13 were waited for; matrix products, arithmetic and copies ran while one was open for 0% of the time, Pallas kernels for 0%

commit v1 on v0

--- a/solution.py
+++ b/solution.py
@@ -33,7 +33,9 @@
         from_prior = passed_along(products[0], "blk", 1)
         raw_factor = jnp.stack([products[0] - from_next, from_prior - products[1]])
         gram = jnp.einsum("ekr,elr->ekl", raw_factor, raw_factor, precision=lax.Precision.HIGHEST)
-        gram = lax.psum(gram, "shard")
+        gram = gram
+        for hop in (1, 2):
+            gram = gram + lax.ppermute(gram, "shard", [(dev, dev ^ hop) for dev in range(4)])
         lower_factor = jnp.linalg.cholesky(gram)
         basis = jax.vmap(lower_solve)(lower_factor, raw_factor)
         left_rows = basis.astype(jnp.bfloat16)

time: 364 us -> 341 us (0.937)
  blocking collectives: 90.5 us -> 48.6 us
  waiting for transfers between devices: 127 us -> 144 us
    psum x4 -> x0, blocking collectives: 41.9 us -> none  [on_device(): gram = lax.psum(gram, 'shard')]
    ppermute x0 -> x8, waiting for transfers between devices: none -> 17.6 us  [on_device(): lax.ppermute(gram, 'shard', [(dev, dev ^ hop) for dev in range(4)])]
  transfers between devices with their start and end apart: 18 -> 26, of which waited for: 13 -> 19; matrix products, arithmetic and copies ran while one was open for 0% -> 0% of each run, Pallas kernels for 0% -> 0%
where the time goes in v1:
time: 341 us; the launch traced here: 340 us
  waiting for transfers between devices  144 us (42%)
  matrix products  55.7 us (16%)
  other arithmetic  48.6 us (14%)
  blocking collectives  48.6 us (14%)
  starting transfers between devices  27.4 us (8%)
  between operations  14.3 us (4%)
    ppermute x17, waiting for transfers between devices, passed_along(): lax.ppermute(value, axis, [(i, (i + by) % peers) for i in range(peers)])  92.8 us
    psum x3, blocking collectives, on_device(): lax.psum(jnp.stack([partials[0] - next_part, prior_part - partials[1]]),...  48.6 us
    psum x1, waiting for transfers between devices, on_device(): lax.psum(jnp.stack([partials[0] - next_part, prior_part - partials[1]]),...  33.4 us
    ppermute x17, starting transfers between devices, passed_along(): lax.ppermute(value, axis, [(i, (i + by) % peers) for i in range(peers)])  24.3 us
    dot_general x4, matrix products, on_device(): jnp.einsum('ekc,rc->ekr', rounded, local_weight, preferred_element_type=j...  24.1 us
    another operation x13, other arithmetic, on_device(): lower_factor = jnp.linalg.cholesky(gram)  24.1 us
    another operation x9, other arithmetic, lower_solve(): jax.scipy.linalg.solve_triangular(lower_factor, right_hand, lower=True)  20 us
    dot_general x4, matrix products, on_device(): jnp.einsum('ekr,rc->ekc', left_rows, local_weight, preferred_element_type...  19.8 us
  transfers between devices with their start and end apart: 26, of which 19 were waited for; matrix products, arithmetic and copies ran while one was open for 0% of the time, Pallas kernels for 0%

profile of v1, /device:TPU:0, one launch (start us, length us, event | category | flops | bytes accessed | tf_op | source)
XLA Modules:
  0.0 340.4 jit_solution(17551521771553519867)
XLA Ops:
  12.2 5.6 %collective-permute-done = bf16[32,2048]{1,0:T(8,128)(2,1)S(1)} collective-permute-done((bf16[32,2048]{1,0:T(8,128)(2,1)S(1)}, bf16[32,2048]{1,0:T(8,128)(2,1)S(1)}, u32[]{:S(2)}, u32[]{:S(2)}) %collective-permute-start) | collective-permute-done | bytes 131104 | tf_op jit(solution)/shard_map/ppermute | solution.py:12
  17.7 6.0 %fusion.14 = f32[2,32,2048]{2,1,0:T(8,128)S(1)} fusion(bf16[1,2048,2048]{2,1,0:T(8,128)(2,1)} %param.5, bf16[1,32,2048]{2,1,0:T(8,128)(2,1)S(1)} %bitcast.173, bf16[1,32,2048]{2,1,0:T(8,128)(2,1)S(1)} %convert_element_type.38), kind=kOutput, calls=%fused_computation.15 | convolution fusion | flops 537001984 | bytes 9175040 | tf_op jit(solution)/shard_map/ekc,rc->ekr/dot_general | solution.py:29
  25.9 11.1 %collective-permute-done.1 = f32[32,2048]{1,0:T(8,128)S(1)} collective-permute-done((f32[32,2048]{1,0:T(8,128)S(1)}, f32[32,2048]{1,0:T(8,128)S(1)}, u32[]{:S(2)}, u32[]{:S(2)}) %collective-permute-start.1) | collective-permute-done | bytes 262176 | tf_op jit(solution)/shard_map/ppermute | solution.py:12
  42.9 5.9 %custom-call.12 = f32[2,32,32]{2,1,0:T(8,128)S(1)} custom-call(f32[2,32,32]{2,1,0:T(8,128)S(1)} %fusion.41), custom_call_target="Cholesky" | custom-call | tf_op jit(solution)/shard_map/jit(cholesky)/cholesky | solution.py:39
  62.2 10.3 %collective-permute-done.5 = f32[32,2048]{1,0:T(8,128)S(1)} collective-permute-done((f32[32,2048]{1,0:T(8,128)S(1)}, f32[32,2048]{1,0:T(8,128)S(1)}, u32[]{:S(2)}, u32[]{:S(2)}) %collective-permute-start.5) | collective-permute-done | bytes 262176 | tf_op jit(solution)/shard_map/ppermute | solution.py:12
  72.6 16.2 %all-reduce.6 = bf16[2,32,2048]{2,1,0:T(8,128)(2,1)S(1)} all-reduce(f32[2,32,2048]{2,1,0:T(8,128)S(1)} %pad_maximum_fusion.1), channel_id=1, replica_groups=mesh['blk'=8,'shard'=4] {'shard'}, use_global_device_ids=true, to_apply=%region_2.0 | all-reduce | flops 131072 | bytes 786432 | tf_op jit(solution)/shard_map/psum | solution.py:47
  88.8 6.0 %fusion.10 = f32[2,32,2048]{2,1,0:T(8,128)S(1)} fusion(bf16[1,2048,2048]{2,1,0:T(8,128)(2,1)} %param.5, bf16[2,32,2048]{2,1,0:T(8,128)(2,1)S(1)} %all-reduce.6), kind=kOutput, calls=%fused_computation.11 | convolution fusion | flops 536870912 | bytes 9175040 | tf_op jit(solution)/shard_map/ekc,rc->ekr/dot_general | solution.py:29
  97.7 11.2 %collective-permute-done.7 = f32[32,2048]{1,0:T(8,128)S(1)} collective-permute-done((f32[32,2048]{1,0:T(8,128)S(1)}, f32[32,2048]{1,0:T(8,128)S(1)}, u32[]{:S(2)}, u32[]{:S(2)}) %collective-permute-start.7) | collective-permute-done | bytes 262176 | tf_op jit(solution)/shard_map/ppermute | solution.py:12
  114.8 5.9 %custom-call.14 = f32[2,32,32]{2,1,0:T(8,128)S(1)} custom-call(f32[2,32,32]{2,1,0:T(8,128)S(1)} %fusion.39), custom_call_target="Cholesky" | custom-call | tf_op jit(solution)/shard_map/jit(cholesky)/cholesky | solution.py:39
  126.5 5.0 %fusion.8 = f32[2,32,2048]{2,1,0:T(8,128)S(1)} fusion(bf16[2,32,2048]{2,1,0:T(8,128)(2,1)S(1)} %convolution_convert_fusion.2, bf16[1,2048,2048]{2,1,0:T(8,128)(2,1)} %param.5), kind=kOutput, calls=%fused_computation.9 | convolution fusion | flops 536870912 | bytes 9175040 | tf_op jit(solution)/shard_map/ekr,rc->ekc/dot_general | solution.py:42
  134.3 10.1 %collective-permute-done.11 = f32[32,2048]{1,0:T(8,128)S(1)} collective-permute-done((f32[32,2048]{1,0:T(8,128)S(1)}, f32[32,2048]{1,0:T(8,128)S(1)}, u32[]{:S(2)}, u32[]{:S(2)}) %collective-permute-start.11) | collective-permute-done | bytes 262176 | tf_op jit(solution)/shard_map/ppermute | solution.py:12
  144.5 16.4 %all-reduce.7 = bf16[2,32,2048]{2,1,0:T(8,128)(2,1)S(1)} all-reduce(f32[2,32,2048]{2,1,0:T(8,128)S(1)} %pad_maximum_fusion.3), channel_id=1, replica_groups=mesh['blk'=8,'shard'=4] {'shard'}, use_global_device_ids=true, to_apply=%region_3.0 | all-reduce | flops 131072 | bytes 786432 | tf_op jit(solution)/shard_map/psum | solution.py:47
  160.9 6.0 %fusion.6 = f32[2,32,2048]{2,1,0:T(8,128)S(1)} fusion(bf16[1,2048,2048]{2,1,0:T(8,128)(2,1)} %param.5, bf16[2,32,2048]{2,1,0:T(8,128)(2,1)S(1)} %all-reduce.7), kind=kOutput, calls=%fused_computation.7 | convolution fusion | flops 536870912 | bytes 9175040 | tf_op jit(solution)/shard_map/ekc,rc->ekr/dot_general | solution.py:29
  169.9 11.5 %collective-permute-done.13 = f32[32,2048]{1,0:T(8,128)S(1)} collective-permute-done((f32[32,2048]{1,0:T(8,128)S(1)}, f32[32,2048]{1,0:T(8,128)S(1)}, u32[]{:S(2)}, u32[]{:S(2)}) %collective-permute-start.13) | collective-permute-done | bytes 262176 | tf_op jit(solution)/shard_map/ppermute | solution.py:12
  187.4 5.9 %custom-call.16 = f32[2,32,32]{2,1,0:T(8,128)S(1)} custom-call(f32[2,32,32]{2,1,0:T(8,128)S(1)} %fusion.37), custom_call_target="Cholesky" | custom-call | tf_op jit(solution)/shard_map/jit(cholesky)/cholesky | solution.py:39
  199.0 5.0 %fusion.4 = f32[2,32,2048]{2,1,0:T(8,128)S(1)} fusion(bf16[2,32,2048]{2,1,0:T(8,128)(2,1)S(1)} %convolution_convert_fusion.1, bf16[1,2048,2048]{2,1,0:T(8,128)(2,1)} %param.5), kind=kOutput, calls=%fused_computation.5 | convolution fusion | flops 536870912 | bytes 9175040 | tf_op jit(solution)/shard_map/ekr,rc->ekc/dot_general | solution.py:42
  206.1 10.9 %collective-permute-done.17 = f32[32,2048]{1,0:T(8,128)S(1)} collective-permute-done((f32[32,2048]{1,0:T(8,128)S(1)}, f32[32,2048]{1,0:T(8,128)S(1)}, u32[]{:S(2)}, u32[]{:S(2)}) %collective-permute-start.17) | collective-permute-done | bytes 262176 | tf_op jit(solution)/shard_map/ppermute | solution.py:12
  217.1 15.9 %all-reduce.8 = bf16[2,32,2048]{2,1,0:T(8,128)(2,1)S(1)} all-reduce(f32[2,32,2048]{2,1,0:T(8,128)S(1)} %pad_maximum_fusion.5), channel_id=1, replica_groups=mesh['blk'=8,'shard'=4] {'shard'}, use_global_device_ids=true, to_apply=%region_4.7 | all-reduce | flops 131072 | bytes 786432 | tf_op jit(solution)/shard_map/psum | solution.py:47
  233.1 6.0 %fusion.2 = f32[2,32,2048]{2,1,0:T(8,128)S(1)} fusion(bf16[1,2048,2048]{2,1,0:T(8,128)(2,1)} %param.5, bf16[2,32,2048]{2,1,0:T(8,128)(2,1)S(1)} %all-reduce.8), kind=kOutput, calls=%fused_computation.3 | convolution fusion | flops 536870912 | bytes 9175040 | tf_op jit(solution)/shard_map/ekc,rc->ekr/dot_general | solution.py:29
  242.1 11.4 %collective-permute-done.19 = f32[32,2048]{1,0:T(8,128)S(1)} collective-permute-done((f32[32,2048]{1,0:T(8,128)S(1)}, f32[32,2048]{1,0:T(8,128)S(1)}, u32[]{:S(2)}, u32[]{:S(2)}) %collective-permute-start.19) | collective-permute-done | bytes 262176 | tf_op jit(solution)/shard_map/ppermute | solution.py:12
  259.5 5.9 %custom-call.18 = f32[2,32,32]{2,1,0:T(8,128)S(1)} custom-call(f32[2,32,32]{2,1,0:T(8,128)S(1)} %fusion.35), custom_call_target="Cholesky" | custom-call | tf_op jit(solution)/shard_map/jit(cholesky)/cholesky | solution.py:39
  279.1 10.7 %collective-permute-done.23 = f32[32,2048]{1,0:T(8,128)S(1)} collective-permute-done((f32[32,2048]{1,0:T(8,128)S(1)}, f32[32,2048]{1,0:T(8,128)S(1)}, u32[]{:S(2)}, u32[]{:S(2)}) %collective-permute-start.23) | collective-permute-done | bytes 262176 | tf_op jit(solution)/shard_map/ppermute | solution.py:12
  290.8 33.4 %all-reduce.5.cloned.1.call-done = f32[2,32,2048]{2,1,0:T(8,128)} async-done(((f32[2,32,2048]{2,1,0:T(8,128)}), f32[2,32,2048]{2,1,0:T(8,128)}) %all-reduce.5.cloned.1.call-update) | async-done | bytes 524304 | tf_op jit(solution)/shard_map/psum | solution.py:47
  325.2 6.9 %fusion.16 = bf16[1,2048,2048]{2,1,0:T(8,128)(2,1)} fusion(bf16[1,2048,2048]{2,1,0:T(8,128)(2,1)} %param.5, bf16[32,2048]{1,0:T(8,128)(2,1)S(1)} %get-tuple-element.39, bf16[32,2048]{1,0:T(8,128)(2,1)S(1)} %get-tuple-element.38, bf16[32,2048]{1,0:T(8,128)(2,1)S(1)} %get-tuple-element.37, bf16[32,2048]{1,0:T(8,128)(2,1)S(1)} %get-tuple-element.36), kind=kOutput, calls=%fused_computation.17 | convolution fusion | flops 554696704 | bytes 17301504 | tf_op jit(solution)/shard_map/jr,jc->rc/dot_general | solution.py:54
  (113 shorter events, 87.1 us)
Async XLA Ops:
  7.2 317.0 %all-reduce.5.cloned.1.call-start = ((), (), s32[]{:S(2)}) async-start(), calls=%async_computation | async-start | bytes 1048576 | tf_op jit(solution)/shard_map/psum | solution.py:47
  8.2 9.6 %collective-permute-start = (bf16[32,2048]{1,0:T(8,128)(2,1)S(1)}, bf16[32,2048]{1,0:T(8,128)(2,1)S(1)}, u32[]{:S(2)}, u32[]{:S(2)}) collective-permute-start(bf16[32,2048]{1,0:T(8,128)(2,1)S(1)} %convert_bitcast_fusion), channel_id=1, source_target_pairs={{0,4},{4,8},{8,12},{12,16},{16,20},{20,24},{24,28},{28,0},{1,5},{5... | collective-permute-start | bytes 393224 | tf_op jit(solution)/shard_map/ppermute | solution.py:12
  23.8 13.2 %collective-permute-start.1 = (f32[32,2048]{1,0:T(8,128)S(1)}, f32[32,2048]{1,0:T(8,128)S(1)}, u32[]{:S(2)}, u32[]{:S(2)}) collective-permute-start(f32[32,2048]{1,0:T(8,128)S(1)} %get-tuple-element.34), channel_id=1, source_target_pairs={{0,28},{4,0},{8,4},{12,8},{16,12},{20,16},{24,20},{28,24},{1,29},{... | collective-permute-start | bytes 786440 | tf_op jit(solution)/shard_map/ppermute | solution.py:12
  25.6 11.4 %collective-permute-start.2 = (f32[32,2048]{1,0:T(8,128)S(1)}, f32[32,2048]{1,0:T(8,128)S(1)}, u32[]{:S(2)}, u32[]{:S(2)}) collective-permute-start(f32[32,2048]{1,0:T(8,128)S(1)} %get-tuple-element.35), channel_id=1, source_target_pairs={{0,4},{4,8},{8,12},{12,16},{16,20},{20,24},{24,28},{28,0},{1,5},{5... | collective-permute-start | bytes 786440 | tf_op jit(solution)/shard_map/ppermute | solution.py:12
  37.6 1.3 collective-permute-start.3
  38.9 3.9 %collective-permute-start.4 = (f32[2,32,32]{1,2,0:T(8,128)S(1)}, f32[2,32,32]{1,2,0:T(8,128)S(1)}, u32[]{:S(2)}, u32[]{:S(2)}) collective-permute-start(f32[2,32,32]{1,2,0:T(8,128)S(1)} %add.47), channel_id=1, source_target_pairs={{0,2},{1,3},{2,0},{3,1},{4,6},{5,7},{6,4},{7,5},{8,10},{9,11},{10,... | collective-permute-start | bytes 24584 | tf_op jit(solution)/shard_map/ppermute | solution.py:38
  59.6 12.9 %collective-permute-start.5 = (f32[32,2048]{1,0:T(8,128)S(1)}, f32[32,2048]{1,0:T(8,128)S(1)}, u32[]{:S(2)}, u32[]{:S(2)}) collective-permute-start(f32[32,2048]{1,0:T(8,128)S(1)} %get-tuple-element.30), channel_id=1, source_target_pairs={{0,28},{4,0},{8,4},{12,8},{16,12},{20,16},{24,20},{28,24},{1,29},{... | collective-permute-start | bytes 786440 | tf_op jit(solution)/shard_map/ppermute | solution.py:12
  62.2 10.3 %collective-permute-start.6 = (f32[32,2048]{1,0:T(8,128)S(1)}, f32[32,2048]{1,0:T(8,128)S(1)}, u32[]{:S(2)}, u32[]{:S(2)}) collective-permute-start(f32[32,2048]{1,0:T(8,128)S(1)} %get-tuple-element.31), channel_id=1, source_target_pairs={{0,4},{4,8},{8,12},{12,16},{16,20},{20,24},{24,28},{28,0},{1,5},{5... | collective-permute-start | bytes 786440 | tf_op jit(solution)/shard_map/ppermute | solution.py:12
  94.9 14.0 %collective-permute-start.7 = (f32[32,2048]{1,0:T(8,128)S(1)}, f32[32,2048]{1,0:T(8,128)S(1)}, u32[]{:S(2)}, u32[]{:S(2)}) collective-permute-start(f32[32,2048]{1,0:T(8,128)S(1)} %get-tuple-element.26), channel_id=1, source_target_pairs={{0,28},{4,0},{8,4},{12,8},{16,12},{20,16},{24,20},{28,24},{1,29},{... | collective-permute-start | bytes 786440 | tf_op jit(solution)/shard_map/ppermute | solution.py:12
  97.7 11.2 %collective-permute-start.8 = (f32[32,2048]{1,0:T(8,128)S(1)}, f32[32,2048]{1,0:T(8,128)S(1)}, u32[]{:S(2)}, u32[]{:S(2)}) collective-permute-start(f32[32,2048]{1,0:T(8,128)S(1)} %get-tuple-element.27), channel_id=1, source_target_pairs={{0,4},{4,8},{8,12},{12,16},{16,20},{20,24},{24,28},{28,0},{1,5},{5... | collective-permute-start | bytes 786440 | tf_op jit(solution)/shard_map/ppermute | solution.py:12
  109.5 1.3 collective-permute-start.9
  110.8 3.9 %collective-permute-start.10 = (f32[2,32,32]{1,2,0:T(8,128)S(1)}, f32[2,32,32]{1,2,0:T(8,128)S(1)}, u32[]{:S(2)}, u32[]{:S(2)}) collective-permute-start(f32[2,32,32]{1,2,0:T(8,128)S(1)} %add.49), channel_id=1, source_target_pairs={{0,2},{1,3},{2,0},{3,1},{4,6},{5,7},{6,4},{7,5},{8,10},{9,11},{10,... | collective-permute-start | bytes 24584 | tf_op jit(solution)/shard_map/ppermute | solution.py:38
  131.5 12.9 %collective-permute-start.11 = (f32[32,2048]{1,0:T(8,128)S(1)}, f32[32,2048]{1,0:T(8,128)S(1)}, u32[]{:S(2)}, u32[]{:S(2)}) collective-permute-start(f32[32,2048]{1,0:T(8,128)S(1)} %get-tuple-element.22), channel_id=1, source_target_pairs={{0,28},{4,0},{8,4},{12,8},{16,12},{20,16},{24,20},{28,24},{1,29},{... | collective-permute-start | bytes 786440 | tf_op jit(solution)/shard_map/ppermute | solution.py:12
  134.3 10.1 %collective-permute-start.12 = (f32[32,2048]{1,0:T(8,128)S(1)}, f32[32,2048]{1,0:T(8,128)S(1)}, u32[]{:S(2)}, u32[]{:S(2)}) collective-permute-start(f32[32,2048]{1,0:T(8,128)S(1)} %get-tuple-element.23), channel_id=1, source_target_pairs={{0,4},{4,8},{8,12},{12,16},{16,20},{20,24},{24,28},{28,0},{1,5},{5... | collective-permute-start | bytes 786440 | tf_op jit(solution)/shard_map/ppermute | solution.py:12
  167.0 14.4 %collective-permute-start.13 = (f32[32,2048]{1,0:T(8,128)S(1)}, f32[32,2048]{1,0:T(8,128)S(1)}, u32[]{:S(2)}, u32[]{:S(2)}) collective-permute-start(f32[32,2048]{1,0:T(8,128)S(1)} %get-tuple-element.18), channel_id=1, source_target_pairs={{0,28},{4,0},{8,4},{12,8},{16,12},{20,16},{24,20},{28,24},{1,29},{... | collective-permute-start | bytes 786440 | tf_op jit(solution)/shard_map/ppermute | solution.py:12
  169.9 11.5 %collective-permute-start.14 = (f32[32,2048]{1,0:T(8,128)S(1)}, f32[32,2048]{1,0:T(8,128)S(1)}, u32[]{:S(2)}, u32[]{:S(2)}) collective-permute-start(f32[32,2048]{1,0:T(8,128)S(1)} %get-tuple-element.19), channel_id=1, source_target_pairs={{0,4},{4,8},{8,12},{12,16},{16,20},{20,24},{24,28},{28,0},{1,5},{5... | collective-permute-start | bytes 786440 | tf_op jit(solution)/shard_map/ppermute | solution.py:12
  183.4 3.9 %collective-permute-start.16 = (f32[2,32,32]{1,2,0:T(8,128)S(1)}, f32[2,32,32]{1,2,0:T(8,128)S(1)}, u32[]{:S(2)}, u32[]{:S(2)}) collective-permute-start(f32[2,32,32]{1,2,0:T(8,128)S(1)} %add.51), channel_id=1, source_target_pairs={{0,2},{1,3},{2,0},{3,1},{4,6},{5,7},{6,4},{7,5},{8,10},{9,11},{10,... | collective-permute-start | bytes 24584 | tf_op jit(solution)/shard_map/ppermute | solution.py:38
  204.0 13.0 %collective-permute-start.17 = (f32[32,2048]{1,0:T(8,128)S(1)}, f32[32,2048]{1,0:T(8,128)S(1)}, u32[]{:S(2)}, u32[]{:S(2)}) collective-permute-start(f32[32,2048]{1,0:T(8,128)S(1)} %get-tuple-element.14), channel_id=1, source_target_pairs={{0,28},{4,0},{8,4},{12,8},{16,12},{20,16},{24,20},{28,24},{1,29},{... | collective-permute-start | bytes 786440 | tf_op jit(solution)/shard_map/ppermute | solution.py:12
  205.7 11.3 %collective-permute-start.18 = (f32[32,2048]{1,0:T(8,128)S(1)}, f32[32,2048]{1,0:T(8,128)S(1)}, u32[]{:S(2)}, u32[]{:S(2)}) collective-permute-start(f32[32,2048]{1,0:T(8,128)S(1)} %get-tuple-element.15), channel_id=1, source_target_pairs={{0,4},{4,8},{8,12},{12,16},{16,20},{20,24},{24,28},{28,0},{1,5},{5... | collective-permute-start | bytes 786440 | tf_op jit(solution)/shard_map/ppermute | solution.py:12
  239.2 14.4 %collective-permute-start.19 = (f32[32,2048]{1,0:T(8,128)S(1)}, f32[32,2048]{1,0:T(8,128)S(1)}, u32[]{:S(2)}, u32[]{:S(2)}) collective-permute-start(f32[32,2048]{1,0:T(8,128)S(1)} %get-tuple-element.10), channel_id=1, source_target_pairs={{0,28},{4,0},{8,4},{12,8},{16,12},{20,16},{24,20},{28,24},{1,29},{... | collective-permute-start | bytes 786440 | tf_op jit(solution)/shard_map/ppermute | solution.py:12
  242.1 11.5 %collective-permute-start.20 = (f32[32,2048]{1,0:T(8,128)S(1)}, f32[32,2048]{1,0:T(8,128)S(1)}, u32[]{:S(2)}, u32[]{:S(2)}) collective-permute-start(f32[32,2048]{1,0:T(8,128)S(1)} %get-tuple-element.11), channel_id=1, source_target_pairs={{0,4},{4,8},{8,12},{12,16},{16,20},{20,24},{24,28},{28,0},{1,5},{5... | collective-permute-start | bytes 786440 | tf_op jit(solution)/shard_map/ppermute | solution.py:12
  255.5 3.9 %collective-permute-start.22 = (f32[2,32,32]{1,2,0:T(8,128)S(1)}, f32[2,32,32]{1,2,0:T(8,128)S(1)}, u32[]{:S(2)}, u32[]{:S(2)}) collective-permute-start(f32[2,32,32]{1,2,0:T(8,128)S(1)} %add.53), channel_id=1, source_target_pairs={{0,2},{1,3},{2,0},{3,1},{4,6},{5,7},{6,4},{7,5},{8,10},{9,11},{10,... | collective-permute-start | bytes 24584 | tf_op jit(solution)/shard_map/ppermute | solution.py:38
  276.2 13.6 %collective-permute-start.23 = (f32[32,2048]{1,0:T(8,128)S(1)}, f32[32,2048]{1,0:T(8,128)S(1)}, u32[]{:S(2)}, u32[]{:S(2)}) collective-permute-start(f32[32,2048]{1,0:T(8,128)S(1)} %get-tuple-element.6), channel_id=1, source_target_pairs={{0,28},{4,0},{8,4},{12,8},{16,12},{20,16},{24,20},{28,24},{1,29},{... | collective-permute-start | bytes 786440 | tf_op jit(solution)/shard_map/ppermute | solution.py:12
  279.1 10.7 %collective-permute-start.24 = (f32[32,2048]{1,0:T(8,128)S(1)}, f32[32,2048]{1,0:T(8,128)S(1)}, u32[]{:S(2)}, u32[]{:S(2)}) collective-permute-start(f32[32,2048]{1,0:T(8,128)S(1)} %get-tuple-element.7), channel_id=1, source_target_pairs={{0,4},{4,8},{8,12},{12,16},{16,20},{20,24},{24,28},{28,0},{1,5},{5... | collective-permute-start | bytes 786440 | tf_op jit(solution)/shard_map/ppermute | solution.py:12
  (2 other events, 2.5 us)
Sparse Core Ops, SparseCore 0:
  290.9 33.2 all-reduce.4
